TPU v7x, 32 devices: a whole 2x2x4 slice. The times are simulated.
32 devices in a mesh: groups: 2 (over y), scan: 4 (over z), stripe: 2 (over x), sub: 2 (over core).
Axes of the slice: x: 2, y: 2, z: 4, core: 2. Of those that a mesh axis runs over, the one named last changes fastest.
Arguments:
- object_field: float32 [2, 2048, 1024], P(None, ('groups', 'stripe', 'sub'), 'scan'), parts along dimension 1, may hold values from -6 to 6
- probe_field: float32 [2, 256, 128], P(None, 'groups'), parts along dimension 1, may hold values from -6 to 6
- intensity: float32 [512, 128, 128], P(('groups', 'scan', 'stripe', 'sub')), parts along dimension 0, may hold values from 0 to 2
- positions: int32 [512, 2], P(('groups', 'scan', 'stripe', 'sub')), parts along dimension 0, may hold values from 0 to 128
- owner_tile: int32 [512, 1], P(('groups', 'scan', 'stripe', 'sub')), parts along dimension 0, may hold values from 0 to 3; in each aligned block of 16 rows (0 to 15, 16 to 31, ...) at most 8 rows name the same one
Outputs:
- object_grad: float32 [2, 2048, 1024], P(None, ('groups', 'stripe', 'sub'), 'scan'), parts along dimension 1
- probe_grad: float32 [2, 256, 128], P(None, 'groups'), parts along dimension 1
There are 2 independent parts, one for each index of `groups`. A program takes and returns all parts, laid end to end along the dimension named above; each array names one. Nothing has to cross between parts.
Inputs may be any that keep to these rules, and one draw needn't show every extreme that they name: `owner_tile`: among the 16 patterns of one device no tile column is named more than 8 times, and on some device one column is named exactly 8 times. `positions`: every window lies wholly inside its owning tile.
All inputs are finite; a program needn't handle non-finite values.
Results may differ from a plain program's by a relative error of at most 0.0001.
Values sent between devices are 32-bit elements; how exact they have to be, the bound alone decides.
A program may use at most 64 MiB of HBM per device.

v0:
```python
import math

import jax
import jax.numpy as jnp
from jax import lax
from jax.sharding import PartitionSpec as P


def tables(extent):
    counter = jnp.arange(extent, dtype=jnp.int32)
    product_mod = counter[:, None] * counter[None, :] % extent
    angles = product_mod.astype(jnp.float32) * (2.0 * math.pi / extent)
    factor = 1.0 / math.sqrt(extent)
    return (jnp.cos(angles) * factor, -jnp.sin(angles) * factor)


def transform(real_in, imag_in, table_re, table_im):
    highest = lax.Precision.HIGHEST
    left_re = jnp.einsum("kn,bnm->bkm", table_re, real_in, precision=highest) - jnp.einsum(
        "kn,bnm->bkm", table_im, imag_in, precision=highest
    )
    left_im = jnp.einsum("kn,bnm->bkm", table_re, imag_in, precision=highest) + jnp.einsum(
        "kn,bnm->bkm", table_im, real_in, precision=highest
    )
    out_re = jnp.einsum("bkm,lm->bkl", left_re, table_re, precision=highest) - jnp.einsum(
        "bkm,lm->bkl", left_im, table_im, precision=highest
    )
    out_im = jnp.einsum("bkm,lm->bkl", left_re, table_im, precision=highest) + jnp.einsum(
        "bkm,lm->bkl", left_im, table_re, precision=highest
    )
    return (out_re, out_im)


def gradients(windows, probe_field, measured, table_re, table_im):
    crop_re, crop_im = (windows[:, 0], windows[:, 1])
    probe_re, probe_im = (probe_field[0], probe_field[1])
    exit_re = probe_re * crop_re - probe_im * crop_im
    exit_im = probe_re * crop_im + probe_im * crop_re
    far_re, far_im = transform(exit_re, exit_im, table_re, table_im)
    misfit = far_re**2 + far_im**2 - measured
    back_re, back_im = transform(misfit * far_re, misfit * far_im, table_re, -table_im)
    object_term = jnp.stack(
        [probe_re * back_re + probe_im * back_im, probe_re * back_im - probe_im * back_re], axis=1
    )
    probe_term = jnp.stack(
        [crop_re * back_re + crop_im * back_im, crop_re * back_im - crop_im * back_re], axis=1
    )
    return (object_term, probe_term)


def cut_windows(source, starts, extent):

    def single(corner):
        return lax.dynamic_slice(
            source, (jnp.zeros((), jnp.int32), corner[0], corner[1]), (2, extent, extent)
        )

    return jax.vmap(single)(starts)


def paste_all(grad_tile, terms, starts, is_valid):

    def paste_one(index, carried):
        corner = (jnp.zeros((), jnp.int32), starts[index, 0], starts[index, 1])
        current = lax.dynamic_slice(carried, corner, terms.shape[1:])
        return lax.dynamic_update_slice(carried, current + terms[index] * is_valid[index], corner)

    return lax.fori_loop(0, terms.shape[0], paste_one, grad_tile)


def shards(object_field, probe_field, intensity, positions, owner_tile):
    scan_count = lax.axis_size("scan")
    pattern_count = intensity.shape[0]
    extent = probe_field.shape[1]
    capacity = 2 * pattern_count // scan_count
    total_slots = scan_count * capacity
    table_re, table_im = tables(extent)
    target = owner_tile[:, 0]
    same_owner = target[:, None] == target[None, :]
    earlier = jnp.arange(pattern_count)[None, :] < jnp.arange(pattern_count)[:, None]
    rank_in = jnp.sum((same_owner & earlier).astype(jnp.int32), axis=1)
    slot_index = target * capacity + rank_in
    empty_corner = jnp.full((total_slots, 2), -1, jnp.int32)
    wanted = empty_corner.at[slot_index].set(positions).reshape(scan_count, capacity, 2)
    asked = lax.all_to_all(wanted, "scan", split_axis=0, concat_axis=0, tiled=True).reshape(
        total_slots, 2
    )
    is_valid = (asked[:, 0] >= 0).astype(jnp.float32)
    starts = jnp.maximum(asked, 0)
    windows = cut_windows(object_field, starts, extent)
    fetched = lax.all_to_all(
        windows.reshape(scan_count, capacity, 2, extent, extent),
        "scan",
        split_axis=0,
        concat_axis=0,
        tiled=True,
    )
    mine = fetched.reshape(total_slots, 2, extent, extent)[slot_index]
    object_term, probe_term = gradients(mine, probe_field, intensity, table_re, table_im)
    outgoing = (
        jnp.zeros((total_slots, 2, extent, extent), jnp.float32).at[slot_index].set(object_term)
    )
    incoming = lax.all_to_all(
        outgoing.reshape(scan_count, capacity, 2, extent, extent),
        "scan",
        split_axis=0,
        concat_axis=0,
        tiled=True,
    )
    grad_tile = paste_all(
        jnp.zeros_like(object_field),
        incoming.reshape(total_slots, 2, extent, extent),
        starts,
        is_valid,
    )
    probe_local = jnp.sum(probe_term, axis=0)
    probe_grad = lax.psum(probe_local, ("scan", "stripe", "sub")) / pattern_count
    return (grad_tile, probe_grad)


def solution(mesh):
    in_specs = (
        P(None, ("groups", "stripe", "sub"), "scan"),
        P(None, "groups", None),
        P(("groups", "scan", "stripe", "sub"), None, None),
        P(("groups", "scan", "stripe", "sub"), None),
        P(("groups", "scan", "stripe", "sub"), None),
    )
    out_specs = (P(None, ("groups", "stripe", "sub"), "scan"), P(None, "groups", None))
    return jax.shard_map(shards, mesh=mesh, in_specs=in_specs, out_specs=out_specs, check_vma=False)
```

profile of v0, /device:TPU:0, one launch (start us, length us, event | category | flops | bytes accessed | tf_op | source)
XLA Modules:
  0.0 720.0 jit_solution(13849673155613123389)
XLA Ops:
  10.8 6.3 all-to-all-start
  17.1 5.6 all-to-all-done
  22.8 2.5 broadcast_in_dim.10.clone
  25.3 112.6 %while.15 = (s32[]{:T(128)}, f32[2,256,256]{2,1,0:T(8,128)}, s32[32,3]{0,1:T(4,128)S(1)}, f32[32,2,128,128]{3,2,1,0:T(8,128)}, s32[]{:T(128)}) while((s32[]{:T(128)}, f32[2,256,256]{2,1,0:T(8,128)}, s32[32,3]{0,1:T(4,128)S(1)}, f32[32,2,128,128]{3,2,1,0:T(8,128)}, s32[]{:T(128)}) %tuple.55), condition=%wide.while_cond, body=%wide.while_body.sunk | while | flops 2 | bytes 263785 | solution.py:54
  25.9 2.9 bitcast_dynamic-update-slice_fusion.2
  29.4 2.9 bitcast_dynamic-update-slice_fusion.2
  33.0 2.9 bitcast_dynamic-update-slice_fusion.2
  36.5 2.9 bitcast_dynamic-update-slice_fusion.2
  40.0 2.9 bitcast_dynamic-update-slice_fusion.2
  43.5 2.9 bitcast_dynamic-update-slice_fusion.2
  47.0 2.9 bitcast_dynamic-update-slice_fusion.2
  50.6 2.9 bitcast_dynamic-update-slice_fusion.2
  54.1 2.9 bitcast_dynamic-update-slice_fusion.2
  57.6 2.9 bitcast_dynamic-update-slice_fusion.2
  61.1 2.9 bitcast_dynamic-update-slice_fusion.2
  64.6 2.9 bitcast_dynamic-update-slice_fusion.2
  68.2 2.9 bitcast_dynamic-update-slice_fusion.2
  71.7 2.9 bitcast_dynamic-update-slice_fusion.2
  75.2 2.9 bitcast_dynamic-update-slice_fusion.2
  78.7 2.9 bitcast_dynamic-update-slice_fusion.2
  82.2 2.9 bitcast_dynamic-update-slice_fusion.2
  85.8 2.9 bitcast_dynamic-update-slice_fusion.2
  89.3 2.9 bitcast_dynamic-update-slice_fusion.2
  92.8 2.9 bitcast_dynamic-update-slice_fusion.2
  96.3 2.9 bitcast_dynamic-update-slice_fusion.2
  99.8 2.9 bitcast_dynamic-update-slice_fusion.2
  103.4 2.9 bitcast_dynamic-update-slice_fusion.2
  106.9 2.9 bitcast_dynamic-update-slice_fusion.2
  110.4 2.9 bitcast_dynamic-update-slice_fusion.2
  113.9 2.9 bitcast_dynamic-update-slice_fusion.2
  117.4 2.9 bitcast_dynamic-update-slice_fusion.2
  120.9 2.9 bitcast_dynamic-update-slice_fusion.2
  124.4 2.9 bitcast_dynamic-update-slice_fusion.2
  128.0 2.9 bitcast_dynamic-update-slice_fusion.2
  131.5 3.0 bitcast_dynamic-update-slice_fusion.2
  135.0 2.9 bitcast_dynamic-update-slice_fusion.2
  137.9 5.0 all-to-all-start.1
  143.0 92.0 %all-to-all-done.1 = f32[4,8,2,128,128]{4,3,2,1,0:T(8,128)} async-done(((f32[4,8,2,128,128]{4,3,2,1,0:T(8,128)}), f32[4,8,2,128,128]{4,3,2,1,0:T(8,128)}, u32[]{:S(2)}, u32[]{:S(2)}) %all-to-all-start.1) | async-done | bytes 4194336 | tf_op jit(solution)/shard_map/all_to_all | solution.py:91
  235.0 2.9 gather_fusion
  268.3 3.3 add_bitcast_fusion
  272.0 2.5 broadcast_in_dim.10
  274.5 3.7 scatter_fusion
  278.2 5.0 all-to-all-start.2
  284.0 154.4 %all-reduce.2.cloned.1.call-done = f32[2,128,128]{2,1,0:T(8,128)} async-done(((f32[2,128,128]{2,1,0:T(8,128)}), f32[2,128,128]{2,1,0:T(8,128)}) %all-reduce.2.cloned.1.call-update) | async-done | bytes 131088 | tf_op jit(solution)/shard_map/psum | solution.py:117
  440.0 272.3 %while.14 = (s32[]{:T(128)}, f32[2,256,256]{2,1,0:T(8,128)S(1)}, s32[32,2]{0,1:T(2,128)S(1)}, f32[32,2,128,128]{3,2,1,0:T(8,128)}, f32[32]{0:T(128)S(1)}, /*index=5*/s32[]{:T(128)}, s32[]{:T(128)}, s32[]{:T(128)}) while((s32[]{:T(128)}, f32[2,256,256]{2,1,0:T(8,128)S(1)}, s32[32,2]{0,1:T(2,128)S(1)}, f32[32,2,128,128]{3,2,1,0:T(8,128)}, ...), condition=%wide.region_4.5_spmd, body=%wide.region_3.4_spmd.sunk | while | flops 65544 | bytes 655565 | solution.py:68
  446.6 2.4 dynamic_update_slice.8
  455.6 2.5 dynamic_update_slice.8
  676.7 2.4 dynamic_update_slice.8
  (234 shorter events, 202.5 us)
Async XLA Ops:
  10.8 11.9 %all-to-all-start = ((s32[4,8,2]{1,2,0:T(2,128)}), s32[4,8,2]{1,2,0:T(2,128)S(1)}, u32[]{:S(2)}, u32[]{:S(2)}) async-start(s32[4,8,2]{1,2,0:T(2,128)} %copy.69), calls=%async_computation | async-start | bytes 8192 | tf_op jit(solution)/shard_map/all_to_all | solution.py:85
  137.9 5.0 copy-start.3
  137.9 97.0 %all-to-all-start.1 = ((f32[4,8,2,128,128]{4,3,2,1,0:T(8,128)}), f32[4,8,2,128,128]{4,3,2,1,0:T(8,128)}, u32[]{:S(2)}, u32[]{:S(2)}) async-start(f32[4,8,2,128,128]{4,3,2,1,0:T(8,128)} %bitcast.137), calls=%async_computation.1 | async-start | bytes 8388608 | tf_op jit(solution)/shard_map/all_to_all | solution.py:91
  251.9 2.0 copy-start
  278.2 5.0 copy-start.1
  278.2 161.8 %all-to-all-start.2 = ((f32[4,8,2,128,128]{4,3,2,1,0:T(8,128)}), f32[4,8,2,128,128]{4,3,2,1,0:T(8,128)}, u32[]{:S(2)}, u32[]{:S(2)}) async-start(f32[4,8,2,128,128]{4,3,2,1,0:T(8,128)} %bitcast.136), calls=%async_computation.2 | async-start | bytes 8388608 | tf_op jit(solution)/shard_map/all_to_all | solution.py:103
  283.2 155.2 %all-reduce.2.cloned.1.call-start = ((), (), s32[]{:S(2)}) async-start(), calls=%async_computation.3 | async-start | bytes 262144 | tf_op jit(solution)/shard_map/psum | solution.py:117
  712.3 0.8 copy-start.2
Sparse Core Ops, SparseCore 0:
  288.0 150.3 all-reduce.1
where the time goes:
time: 735 us; the launch traced here: 720 us
  waiting for transfers between devices  252 us (34%)
  local copies, waits for them, and re-layouts  229 us (31%)
  loops' own time  119 us (16%)
  other arithmetic  55.9 us (8%)
  matrix products  33.7 us (5%)
  starting transfers between devices  16.3 us (2%)
  between operations  14.3 us (2%)
    psum x1, waiting for transfers between devices, shards(): lax.psum(probe_local, ('scan', 'stripe', 'sub')) / pattern_count  154 us
    another operation x1, loops' own time, paste_all(): return lax.fori_loop(0, terms.shape[0], paste_one, grad_tile)  119 us
    gather x96, local copies, waits for them, and re-layouts  113 us
    all_to_all x1, waiting for transfers between devices, shards(): lax.all_to_all(windows.reshape(scan_count, capacity, 2, extent, extent),...  92 us
    dynamic_update_slice x32, local copies, waits for them, and re-layouts, paste_one(): lax.dynamic_update_slice(carried, current + terms[index] * is_valid[index...  61.9 us
    add x32, other arithmetic, paste_one(): current + terms[index] * is_valid[index]  51.8 us
    dynamic_slice x32, local copies, waits for them, and re-layouts, paste_one(): is_valid[index]  19.8 us
    dynamic_slice x32, local copies, waits for them, and re-layouts, paste_one(): corner = (jnp.zeros((), jnp.int32), starts[index, 0], starts[index, 1])  19.8 us
  transfers between devices with their start and end apart: 4, of which 3 were waited for; matrix products, arithmetic and copies ran while one was open for 0% of the time, Pallas kernels for 0%

commit v1 on v0

v1 whole, which is shorter than its diff:
```python
import functools
import math

import jax
import jax.numpy as jnp
import ml_dtypes
import numpy as np
from jax import lax
from jax.experimental import pallas as pl
from jax.experimental.pallas import tpu as pltpu
from jax.sharding import PartitionSpec as P

MESH = pl.DeviceIdType.MESH


def tables(extent):
    counter = np.arange(extent)
    angles = (counter[:, None] * counter[None, :] % extent) * (2.0 * math.pi / extent)
    c, s = np.cos(angles) / math.sqrt(extent), -np.sin(angles) / math.sqrt(extent)
    parts = []
    for whole in (np.block([[c, s], [-s, c]]), np.block([[c, -s], [s, c]])):
        high = whole.astype(np.float32).astype(ml_dtypes.bfloat16)
        low = (whole - high.astype(np.float64)).astype(np.float32).astype(ml_dtypes.bfloat16)
        parts += [high, low]
    return np.stack(parts)


def split(x):
    high = x.astype(jnp.bfloat16)
    return high, (x - high.astype(jnp.float32)).astype(jnp.bfloat16)


def dot(a, b):
    return jnp.dot(a, b, preferred_element_type=jnp.float32)


def dot_right(x, high, low):
    x_high, x_low = split(x)
    return dot(x_high, high) + dot(x_low, high) + dot(x_high, low)


def dot_left(high, low, x):
    x_high, x_low = split(x)
    return dot(high, x_high) + dot(high, x_low) + dot(low, x_high)


def kernel(
    sizes, table_sm, table_vm, inten, obj, probe, dft, grad, probe_out,
    send, recv, meta_in, meta, field, pad, total, reduced, gathered, arrived,
    send_sem, recv_sem, meta_send_sem, meta_recv_sem, local_sem,
    rs_send, rs_recv, ag_send, ag_recv,
):
    n, stripes, subs, cap, batch, offsets = sizes
    groups = cap // batch
    extent = inten.shape[1]
    tile = obj.shape[1]
    halves = tile // extent
    members = n * stripes * subs
    rows = arrived.shape[1]
    owners = 2 * extent // rows
    my_group, me = lax.axis_index("groups"), lax.axis_index("scan")
    my_stripe, my_sub = lax.axis_index("stripe"), lax.axis_index("sub")
    mine = (me * stripes + my_stripe) * subs + my_sub

    def member(place):
        return (my_group, place // (stripes * subs), place // subs % stripes, place % subs)

    def other(step):
        return lax.rem(mine + step, members)

    barrier = pltpu.get_barrier_semaphore()

    def greet(step, carry):
        pl.semaphore_signal(barrier, inc=1, device_id=member(other(step)), device_id_type=MESH)
        return carry

    lax.fori_loop(1, members, greet, 0)

    def pack(o, target, into):
        def one(slot, carry):
            into[o, slot] = inten[table_sm[target, 0, slot]]
            return carry

        lax.fori_loop(0, cap, one, 0)

    def data_copy(o, g, target):
        part = pl.ds(g * batch, batch)
        return pltpu.make_async_remote_copy(
            src_ref=send.at[o, part], dst_ref=recv.at[o, part],
            send_sem=send_sem, recv_sem=recv_sem.at[o, g],
            device_id=(my_group, target, my_stripe, my_sub), device_id_type=MESH,
        )

    def meta_copy(o, target):
        return pltpu.make_async_remote_copy(
            src_ref=table_vm.at[target], dst_ref=meta_in.at[o],
            send_sem=meta_send_sem, recv_sem=meta_recv_sem.at[o],
            device_id=(my_group, target, my_stripe, my_sub), device_id_type=MESH,
        )

    targets = [lax.rem(me + offset, n) for offset in offsets]
    for o in range(1, n):
        pack(o, targets[o], send)
    pl.semaphore_wait(barrier, members - 1)
    for o in range(1, n):
        meta_copy(o, targets[o]).start()
    for o in range(1, n):
        for g in range(groups):
            data_copy(o, g, targets[o]).start()
    own = pltpu.make_async_copy(table_vm.at[me], meta.at[0], local_sem)
    own.start()
    pack(0, me, recv)
    own.wait()

    for h in range(halves):
        field[:, h] = obj[:, :, h * extent:(h + 1) * extent]
    grad[...] = jnp.zeros_like(grad)
    total[...] = jnp.zeros_like(total)
    pad[...] = jnp.zeros_like(pad)

    def step_of(i, carry):
        o, g = i // groups, i % groups

        @pl.when((o > 0) & (g == 0))
        def _():
            meta_copy(o, me).wait_recv()
            down = pltpu.make_async_copy(meta_in.at[o], meta.at[o], local_sem)
            down.start()
            down.wait()

        @pl.when(o > 0)
        def _():
            data_copy(o, g, me).wait_recv()

        corners, crops, exits = [], [], []
        pr, pi = probe[0], probe[1]
        for b in range(batch):
            slot = g * batch + b
            row, col = meta[o, 0, cap + slot], meta[o, 0, 2 * cap + slot]
            weight = jnp.where(meta[o, 0, 3 * cap + slot] > 0, 1.0, 0.0).astype(jnp.float32)
            corners.append((row, col, weight))
            back_by = lax.rem(tile - col, tile)
            cr, ci = [
                pltpu.roll(
                    jnp.concatenate([field[c, h, pl.ds(row, extent), :] for h in range(halves)], axis=1), back_by, 1
                )[:, :extent]
                for c in range(2)
            ]
            crops.append((cr, ci))
            exits.append(jnp.concatenate([pr * cr - pi * ci, pr * ci + pi * cr], axis=1))
        y = dot_right(jnp.concatenate(exits, axis=0), dft[0], dft[1])

        def turn(x):
            return jnp.concatenate(
                [
                    jnp.concatenate(
                        [x[b * extent:(b + 1) * extent, c * extent:(c + 1) * extent] for b in range(batch)], axis=1
                    )
                    for c in range(2)
                ],
                axis=0,
            )

        z = dot_left(dft[2], dft[3], turn(y))
        re, im = z[:extent], z[extent:]
        measured = jnp.concatenate([recv[o, g * batch + b] for b in range(batch)], axis=1)
        misfit = re * re + im * im - measured
        v = dot_left(dft[0], dft[1], jnp.concatenate([misfit * re, misfit * im], axis=0))
        turned = jnp.concatenate(
            [
                jnp.concatenate(
                    [v[c * extent:(c + 1) * extent, b * extent:(b + 1) * extent] for c in range(2)], axis=1
                )
                for b in range(batch)
            ],
            axis=0,
        )
        back = dot_right(turned, dft[2], dft[3])
        sum_re, sum_im = total[:extent], total[extent:]
        nothing = jnp.zeros((extent, tile - extent), jnp.float32)
        for b in range(batch):
            row, col, weight = corners[b]
            cr, ci = crops[b]
            br = back[b * extent:(b + 1) * extent, :extent] * weight
            bi = back[b * extent:(b + 1) * extent, extent:] * weight
            sum_re += cr * br + ci * bi
            sum_im += cr * bi - ci * br
            for c, term in enumerate((pr * br + pi * bi, pr * bi - pi * br)):
                wide = pltpu.roll(jnp.concatenate([term, nothing], axis=1), col, 1)
                for h in range(halves):
                    pad[b, c, h, tile - extent:tile, :] = wide[:, h * extent:(h + 1) * extent]
        total[:extent] = sum_re
        total[extent:] = sum_im
        for c in range(2):
            for start in range(0, tile, 64):
                for h in range(halves):
                    held = grad[c, start:start + 64, h * extent:(h + 1) * extent]
                    for b in range(batch):
                        held += pad[b, c, h, pl.ds(tile - extent - corners[b][0] + start, 64), :]
                    grad[c, start:start + 64, h * extent:(h + 1) * extent] = held
        return carry

    lax.fori_loop(0, n * groups, step_of, 0)

    def when(condition, body):
        if owners == members:
            body()
        else:
            pl.when(condition)(body)

    def part_of(place):
        return pl.ds(pl.multiple_of(place * rows, rows), rows)

    def scatter(step, carry):
        to = other(step)

        def go():
            pltpu.make_async_remote_copy(
                src_ref=total.at[part_of(to)], dst_ref=arrived.at[step - 1], send_sem=rs_send, recv_sem=rs_recv,
                device_id=member(to), device_id_type=MESH,
            ).start()

        when(to < owners, go)
        return carry

    def wait_for(sem, count):
        whole = arrived.at[pl.ds(0, count)]
        pltpu.make_async_copy(whole, whole, sem).wait()

    lax.fori_loop(1, members, scatter, 0)

    def gather():
        wait_for(rs_recv, members - 1)
        held = total[part_of(mine), :]
        held = held + jnp.sum(arrived[...], axis=0)
        reduced[...] = held * (1.0 / inten.shape[0])
        gathered[mine] = reduced[...]

        def tell(step, carry):
            pltpu.make_async_remote_copy(
                src_ref=reduced, dst_ref=gathered.at[mine], send_sem=ag_send, recv_sem=ag_recv,
                device_id=member(other(step)), device_id_type=MESH,
            ).start()
            return carry

        lax.fori_loop(1, members, tell, 0)

    when(mine < owners, gather)
    if owners == members:
        wait_for(ag_recv, members - 1)
        wait_for(rs_send, members - 1)
        wait_for(ag_send, members - 1)
    else:

        @pl.when(mine < owners)
        def _():
            wait_for(ag_recv, owners - 1)
            wait_for(rs_send, owners - 1)
            wait_for(ag_send, members - 1)

        @pl.when(mine >= owners)
        def _():
            wait_for(ag_recv, owners)
            wait_for(rs_send, owners)

    for place in range(owners):
        probe_out[place * rows:(place + 1) * rows] = gathered[place]
    sent = send.at[pl.ds(1, n - 1)]
    pltpu.make_async_copy(sent, sent, send_sem).wait()
    told = meta_in.at[pl.ds(1, n - 1)]
    pltpu.make_async_copy(told, told, meta_send_sem).wait()


def shards(object_field, probe_field, intensity, positions, owner_tile):
    n, stripes, subs = lax.axis_size("scan"), lax.axis_size("stripe"), lax.axis_size("sub")
    count, extent = intensity.shape[0], probe_field.shape[1]
    tile = object_field.shape[1]
    cap = min(count, 2 * count // n)
    batch = min(cap, 4)
    members = n * stripes * subs
    rows = max(8, 2 * extent // members)
    owners = 2 * extent // rows

    owner = owner_tile[:, 0]
    places = jnp.arange(count, dtype=jnp.int32)
    rank = jnp.sum((owner[:, None] == owner[None, :]) & (places[None, :] < places[:, None]), axis=1, dtype=jnp.int32)
    named = jnp.arange(n, dtype=jnp.int32)[:, None, None, None] == owner
    ranked = jnp.arange(cap, dtype=jnp.int32)[:, None] == rank
    facts = jnp.stack([places, positions[:, 0], positions[:, 1], jnp.ones_like(places)])[:, None, :]
    table = jnp.sum(jnp.where(named & ranked, facts, 0), axis=3, dtype=jnp.int32).reshape(n, 1, 4 * cap)
    table = jnp.pad(table, ((0, 0), (0, 0), (0, 128 - 4 * cap)))

    offsets = sorted(range(n), key=lambda o: (o != 0, o))
    vmem = pl.BlockSpec(memory_space=pltpu.VMEM)
    dma = pltpu.SemaphoreType.DMA
    f32 = jnp.float32
    grad, probe_grad = pl.pallas_call(
        functools.partial(kernel, (n, stripes, subs, cap, batch, tuple(offsets))),
        out_shape=(
            jax.ShapeDtypeStruct((2, tile, tile), f32),
            jax.ShapeDtypeStruct((2 * extent, extent), f32),
        ),
        in_specs=[pl.BlockSpec(memory_space=pltpu.SMEM)] + [vmem] * 5,
        out_specs=(vmem, vmem),
        scratch_shapes=[
            pltpu.VMEM((n, cap, extent, extent), f32),
            pltpu.VMEM((n, cap, extent, extent), f32),
            pltpu.VMEM((n, 1, 128), jnp.int32),
            pltpu.SMEM((n, 1, 128), jnp.int32),
            pltpu.VMEM((2, tile // extent, tile, extent), f32),
            pltpu.VMEM((batch, 2, tile // extent, 2 * tile - extent, extent), f32),
            pltpu.VMEM((2 * extent, extent), f32),
            pltpu.VMEM((rows, extent), f32),
            pltpu.VMEM((owners, rows, extent), f32),
            pltpu.VMEM((members - 1, rows, extent), f32),
            dma, dma((n, cap // batch)), dma, dma((n,)), dma, dma, dma, dma, dma,
        ],
        compiler_params=pltpu.CompilerParams(
            collective_id=0, has_side_effects=True, vmem_limit_bytes=40 * 1024 * 1024
        ),
        cost_estimate=pl.CostEstimate(
            flops=3 * 4 * 2 * 256 * 256 * 128 * n * cap, bytes_accessed=8 * 1024 * 1024, transcendentals=0
        ),
    )(table, table, intensity, object_field, probe_field, jnp.asarray(tables(extent)))
    return grad, probe_grad.reshape(2, extent, extent)


def solution(mesh):
    in_specs = (
        P(None, ("groups", "stripe", "sub"), "scan"),
        P(None, "groups", None),
        P(("groups", "scan", "stripe", "sub"), None, None),
        P(("groups", "scan", "stripe", "sub"), None),
        P(("groups", "scan", "stripe", "sub"), None),
    )
    out_specs = (P(None, ("groups", "stripe", "sub"), "scan"), P(None, "groups", None))
    return jax.shard_map(shards, mesh=mesh, in_specs=in_specs, out_specs=out_specs, check_vma=False)
```

time: 735 us -> 79.1 us (0.11); the launches traced: 720 us -> 78.8 us
  waiting for transfers between devices: 252 us -> 0 us
  local copies, waits for them, and re-layouts: 229 us -> 7.16 us
  loops' own time: 119 us -> 0 us
  Pallas kernels: 0 us -> 70.3 us
  other arithmetic: 55.9 us -> 0.63 us
  matrix products: 33.7 us -> 0 us
  starting transfers between devices: 16.3 us -> 0 us
  between operations: 14.3 us -> 0.66 us
    psum x1 -> x0, waiting for transfers between devices: 154 us -> none  [shards(): lax.psum(probe_local, ('scan', 'stripe', 'sub')) / pattern_count]
    another operation x2 -> x0, loops' own time: 119 us -> none  [the longest x1 119 us: paste_all(): return lax.fori_loop(0, terms.shape[0], paste_one, grad_tile)]
    gather x97 -> x0, local copies, waits for them, and re-layouts: 115 us -> none
    all_to_all x3 -> x0, waiting for transfers between devices: 97.6 us -> none  [the longest x1 92 us: shards(): lax.all_to_all(windows.reshape(scan_count, capacity, 2, extent, extent),...]
    pallas_call x0 -> x1, Pallas kernels: none -> 70.3 us  [shards(): pl.pallas_call(functools.partial(kernel, (n, stripes, subs, cap, batch, t...]
    dynamic_update_slice x32 -> x0, local copies, waits for them, and re-layouts: 61.9 us -> none  [paste_one(): lax.dynamic_update_slice(carried, current + terms[index] * is_valid[index...]
    add x32 -> x0, other arithmetic: 51.8 us -> none  [paste_one(): current + terms[index] * is_valid[index]]
    dynamic_slice x64 -> x0, local copies, waits for them, and re-layouts: 39.6 us -> none  [the longest x32 19.8 us: paste_one(): is_valid[index]]
  transfers between devices with their start and end apart: 4 -> 0, of which waited for: 3 -> 0; matrix products, arithmetic and copies ran while one was open for 0% -> 0% of each run, Pallas kernels for 0% -> 0%
where the time goes in v1:
time: 79.1 us; the launch traced here: 78.8 us
  Pallas kernels  70.3 us (89%)
  local copies, waits for them, and re-layouts  7.16 us (9%)
    pallas_call x1, Pallas kernels, shards(): pl.pallas_call(functools.partial(kernel, (n, stripes, subs, cap, batch, t...  70.3 us
    unnamed x14, local copies, waits for them, and re-layouts  6.99 us

profile of v1, /device:TPU:0, one launch (start us, length us, event | category | flops | bytes accessed | tf_op | source)
XLA Modules:
  0.0 78.8 jit_solution(10104689111693576718)
XLA Ops:
  0.6 0.0 copy-start.5
  0.6 0.6 copy-done.5
  1.3 0.2 convert_reduce_fusion
  1.5 0.1 pad.8.clone
  1.6 0.0 copy-start.4
  1.6 0.7 copy-done.4
  2.2 0.1 add_add_fusion
  2.3 0.4 select_reduce_fusion
  2.7 0.1 reshape.62
  2.8 0.0 copy-start
  2.8 1.2 %copy-done = f32[16,128,128]{2,1,0:T(8,128)S(1)} copy-done((f32[16,128,128]{2,1,0:T(8,128)S(1)}, f32[16,128,128]{2,1,0:T(8,128)}, u32[]{:S(2)}) %copy-start) | copy-done | bytes 1048600
  4.0 0.0 copy-start.1
  4.0 1.0 %copy-done.1 = f32[2,256,256]{2,1,0:T(8,128)S(1)} copy-done((f32[2,256,256]{2,1,0:T(8,128)S(1)}, f32[2,256,256]{2,1,0:T(8,128)}, u32[]{:S(2)}) %copy-start.1) | copy-done | bytes 524312
  5.1 0.0 copy-start.2
  5.1 0.9 %copy-done.2 = f32[2,128,128]{2,1,0:T(8,128)S(1)} copy-done((f32[2,128,128]{2,1,0:T(8,128)S(1)}, f32[2,128,128]{2,1,0:T(8,128)}, u32[]{:S(2)}) %copy-start.2) | copy-done | bytes 131096
  6.0 0.0 copy-start.3
  6.0 1.0 %copy-done.3 = bf16[4,256,256]{2,1,0:T(8,128)(2,1)S(1)} copy-done((bf16[4,256,256]{2,1,0:T(8,128)(2,1)S(1)}, bf16[4,256,256]{2,1,0:T(8,128)(2,1)}, u32[]{:S(2)}) %copy-start.3) | copy-done | bytes 524312
  7.0 70.3 %shard_map.77 = (f32[2,256,256]{2,1,0:T(8,128)S(1)}, f32[256,128]{1,0:T(8,128)S(1)}) custom-call(s32[4,1,128]{2,1,0:T(1,128)S(1)} %pad.4.table_sm.table_vm, s32[4,1,128]{2,1,0:T(1,128)S(1)} %pad.4.table_sm.table_vm, f32[16,128,128]{2,1,0:T(8,128)S(1)} %copy-done, f32[2,256,256]{2,1,0:T(8,128)S(1)} %copy-done.1, f32[2,128,128]{2,1,0:T(8,128)S(1)} %copy-done.2, ...), custom_call_target="tpu_custom_call" | custom-call | flops 6442450944 | bytes 8388608 | tf_op jit(solution)/shard_map/pallas_call | solution.py:297
  77.3 0.8 %copy.12 = f32[2,256,256]{2,1,0:T(8,128)} copy(f32[2,256,256]{2,1,0:T(8,128)S(1)} %get-tuple-element.10) | data formatting | bytes 1048576
  78.1 0.7 copy.13
  (6 shorter events, 0.0 us)
Async XLA Ops:
  0.6 0.7 copy-start.5
  1.6 0.7 copy-start.4
  2.8 1.2 %copy-start = (f32[16,128,128]{2,1,0:T(8,128)S(1)}, f32[16,128,128]{2,1,0:T(8,128)}, u32[]{:S(2)}) copy-start(f32[16,128,128]{2,1,0:T(8,128)} %inten.1) | copy-start | bytes 3145732
  4.0 1.0 %copy-start.1 = (f32[2,256,256]{2,1,0:T(8,128)S(1)}, f32[2,256,256]{2,1,0:T(8,128)}, u32[]{:S(2)}) copy-start(f32[2,256,256]{2,1,0:T(8,128)} %obj.1) | copy-start | bytes 1572868
  5.1 0.9 %copy-start.2 = (f32[2,128,128]{2,1,0:T(8,128)S(1)}, f32[2,128,128]{2,1,0:T(8,128)}, u32[]{:S(2)}) copy-start(f32[2,128,128]{2,1,0:T(8,128)} %probe.1) | copy-start | bytes 393220
  6.0 1.0 %copy-start.3 = (bf16[4,256,256]{2,1,0:T(8,128)(2,1)S(1)}, bf16[4,256,256]{2,1,0:T(8,128)(2,1)}, u32[]{:S(2)}) copy-start(bf16[4,256,256]{2,1,0:T(8,128)(2,1)} %constant.6.clone.dft) | copy-start | bytes 1572868

commit v2 on v1

--- a/solution.py
+++ b/solution.py
@@ -3,7 +3,6 @@
 
 import jax
 import jax.numpy as jnp
-import ml_dtypes
 import numpy as np
 from jax import lax
 from jax.experimental import pallas as pl
@@ -11,18 +10,23 @@
 from jax.sharding import PartitionSpec as P
 
 MESH = pl.DeviceIdType.MESH
+AHEAD = 4
 
 
 def tables(extent):
     counter = np.arange(extent)
     angles = (counter[:, None] * counter[None, :] % extent) * (2.0 * math.pi / extent)
-    c, s = np.cos(angles) / math.sqrt(extent), -np.sin(angles) / math.sqrt(extent)
-    parts = []
-    for whole in (np.block([[c, s], [-s, c]]), np.block([[c, -s], [s, c]])):
-        high = whole.astype(np.float32).astype(ml_dtypes.bfloat16)
-        low = (whole - high.astype(np.float64)).astype(np.float32).astype(ml_dtypes.bfloat16)
-        parts += [high, low]
-    return np.stack(parts)
+    return (np.stack([np.cos(angles), -np.sin(angles)]) / math.sqrt(extent)).astype(np.float32)
+
+
+def other_place(me, mask, n):
+    if n & (n - 1):
+        return lax.rem(me + mask, n)
+    place, bit = 0, 1
+    while bit < n:
+        place = place + bit * ((me // bit + mask // bit) % 2)
+        bit *= 2
+    return place
 
 
 def split(x):
@@ -45,12 +49,12 @@
 
 
 def kernel(
-    sizes, table_sm, table_vm, inten, obj, probe, dft, grad, probe_out,
-    send, recv, meta_in, meta, field, pad, total, reduced, gathered, arrived,
-    send_sem, recv_sem, meta_send_sem, meta_recv_sem, local_sem,
+    sizes, places_hbm, owner_hbm, inten_hbm, obj, probe_hbm, waves_hbm, grad, probe_out,
+    inten, probe, waves, dft, send, recv, places_in, owner_in, places, owner, field, pad, total, reduced, gathered, arrived,
+    in_sem, send_sem, recv_sem, meta_send_sem, meta_recv_sem, local_sem,
     rs_send, rs_recv, ag_send, ag_recv,
 ):
-    n, stripes, subs, cap, batch, offsets = sizes
+    n, stripes, subs, cap, batch = sizes
     groups = cap // batch
     extent = inten.shape[1]
     tile = obj.shape[1]
@@ -68,65 +72,124 @@
     def other(step):
         return lax.rem(mine + step, members)
 
+    def each_member(body):
+        lax.fori_loop(1, members, body, 0, unroll=members <= 16)
+
     barrier = pltpu.get_barrier_semaphore()
 
     def greet(step, carry):
         pl.semaphore_signal(barrier, inc=1, device_id=member(other(step)), device_id_type=MESH)
         return carry
 
-    lax.fori_loop(1, members, greet, 0)
-
-    def pack(o, target, into):
-        def one(slot, carry):
-            into[o, slot] = inten[table_sm[target, 0, slot]]
-            return carry
-
-        lax.fori_loop(0, cap, one, 0)
+    own = [
+        pltpu.make_async_copy(places_hbm, places.at[0], local_sem.at[0]),
+        pltpu.make_async_copy(owner_hbm, owner.at[0], local_sem.at[1]),
+    ]
+    for copy in own:
+        copy.start()
+    fetch = pltpu.make_async_copy(inten_hbm, inten, in_sem.at[0])
+    fetch.start()
+    later = [
+        pltpu.make_async_copy(obj.at[:, :, pl.ds(h * extent, extent)], field.at[:, h], in_sem.at[3 + h])
+        for h in range(halves)
+    ]
+    later += [
+        pltpu.make_async_copy(probe_hbm, probe, in_sem.at[1]),
+        pltpu.make_async_copy(waves_hbm, waves, in_sem.at[2]),
+    ]
+    for copy in later:
+        copy.start()
+    each_member(greet)
+
+    def find(o, target, slot):
+        index, seen = jnp.int32(0), jnp.int32(0)
+        for j in range(inten.shape[0]):
+            hit = owner[o, 0, j] == target
+            index = jnp.where(hit & (seen == slot), j, index)
+            seen = seen + jnp.where(hit, 1, 0)
+        return index, seen > slot
+
+    def pack(o, g, target, into):
+        for b in range(batch):
+            slot = g * batch + b
+            into[o, slot] = inten[find(0, target, slot)[0]]
 
     def data_copy(o, g, target):
         part = pl.ds(g * batch, batch)
         return pltpu.make_async_remote_copy(
             src_ref=send.at[o, part], dst_ref=recv.at[o, part],
-            send_sem=send_sem, recv_sem=recv_sem.at[o, g],
+            send_sem=send_sem.at[o, g], recv_sem=recv_sem.at[o, g],
             device_id=(my_group, target, my_stripe, my_sub), device_id_type=MESH,
         )
 
-    def meta_copy(o, target):
-        return pltpu.make_async_remote_copy(
-            src_ref=table_vm.at[target], dst_ref=meta_in.at[o],
-            send_sem=meta_send_sem, recv_sem=meta_recv_sem.at[o],
-            device_id=(my_group, target, my_stripe, my_sub), device_id_type=MESH,
-        )
-
-    targets = [lax.rem(me + offset, n) for offset in offsets]
-    for o in range(1, n):
-        pack(o, targets[o], send)
+    def meta_copies(o, target):
+        return [
+            pltpu.make_async_remote_copy(
+                src_ref=src, dst_ref=dst.at[o],
+                send_sem=meta_send_sem.at[k, o], recv_sem=meta_recv_sem.at[k, o],
+                device_id=(my_group, target, my_stripe, my_sub), device_id_type=MESH,
+            )
+            for k, (src, dst) in enumerate(((places_hbm, places_in), (owner_hbm, owner_in)))
+        ]
+
+    targets = [other_place(me, o, n) for o in range(n)]
+    ahead = min(AHEAD, (n - 1) * groups)
+
+    def turn_of(i):
+        return 1 + (i + 1) % (n - 1), i // (n - 1)
+
+    for copy in own:
+        copy.wait()
+    fetch.wait()
+    pack(*turn_of(0), targets[turn_of(0)[0]], send)
     pl.semaphore_wait(barrier, members - 1)
     for o in range(1, n):
-        meta_copy(o, targets[o]).start()
-    for o in range(1, n):
-        for g in range(groups):
+        for copy in meta_copies(o, targets[o]):
+            copy.start()
+    for i in range((n - 1) * groups):
+        o, g = turn_of(i)
+        if i:
+            pack(o, g, targets[o], send)
+        if i < ahead:
             data_copy(o, g, targets[o]).start()
-    own = pltpu.make_async_copy(table_vm.at[me], meta.at[0], local_sem)
-    own.start()
-    pack(0, me, recv)
-    own.wait()
-
-    for h in range(halves):
-        field[:, h] = obj[:, :, h * extent:(h + 1) * extent]
+    for g in range(groups):
+        pack(0, g, me, recv)
+    for copy in later:
+        copy.wait()
+    for k, sign in enumerate((1.0, -1.0)):
+        c, s = waves[0], waves[1] * sign
+        high, low = split(jnp.concatenate([jnp.concatenate([c, s], 1), jnp.concatenate([-s, c], 1)], 0))
+        dft[2 * k] = high
+        dft[2 * k + 1] = low
+
     grad[...] = jnp.zeros_like(grad)
     total[...] = jnp.zeros_like(total)
     pad[...] = jnp.zeros_like(pad)
 
-    def step_of(i, carry):
-        o, g = i // groups, i % groups
+    def step_of(j, carry):
+        i = j - groups
+        o = jnp.where(i < 0, 0, 1 + (i + 1) % (n - 1))
+        g = jnp.where(i < 0, j, i // (n - 1))
+
+        @pl.when((i >= 0) & (i + ahead < (n - 1) * groups))
+        def _():
+            data_copy(o, g, me).wait_send()
+            next_o, next_g = turn_of(i + ahead)
+            to = other_place(me, next_o, n)
+            data_copy(next_o, next_g, to).start()
 
         @pl.when((o > 0) & (g == 0))
         def _():
-            meta_copy(o, me).wait_recv()
-            down = pltpu.make_async_copy(meta_in.at[o], meta.at[o], local_sem)
-            down.start()
-            down.wait()
+            for copy in meta_copies(o, me):
+                copy.wait_recv()
+            down = [
+                pltpu.make_async_copy(places_in.at[o], places.at[o], local_sem.at[0]),
+                pltpu.make_async_copy(owner_in.at[o], owner.at[o], local_sem.at[1]),
+            ]
+            for copy in down:
+                copy.start()
+            for copy in down:
+                copy.wait()
 
         @pl.when(o > 0)
         def _():
@@ -136,8 +199,9 @@
         pr, pi = probe[0], probe[1]
         for b in range(batch):
             slot = g * batch + b
-            row, col = meta[o, 0, cap + slot], meta[o, 0, 2 * cap + slot]
-            weight = jnp.where(meta[o, 0, 3 * cap + slot] > 0, 1.0, 0.0).astype(jnp.float32)
+            index, is_there = find(o, me, slot)
+            row, col = places[o, 0, index], places[o, 1, index]
+            weight = jnp.where(is_there, 1.0, 0.0).astype(jnp.float32)
             corners.append((row, col, weight))
             back_by = lax.rem(tile - col, tile)
             cr, ci = [
@@ -227,7 +291,7 @@
         whole = arrived.at[pl.ds(0, count)]
         pltpu.make_async_copy(whole, whole, sem).wait()
 
-    lax.fori_loop(1, members, scatter, 0)
+    each_member(scatter)
 
     def gather():
         wait_for(rs_recv, members - 1)
@@ -243,7 +307,7 @@
             ).start()
             return carry
 
-        lax.fori_loop(1, members, tell, 0)
+        each_member(tell)
 
     when(mine < owners, gather)
     if owners == members:
@@ -265,10 +329,11 @@
 
     for place in range(owners):
         probe_out[place * rows:(place + 1) * rows] = gathered[place]
-    sent = send.at[pl.ds(1, n - 1)]
-    pltpu.make_async_copy(sent, sent, send_sem).wait()
-    told = meta_in.at[pl.ds(1, n - 1)]
-    pltpu.make_async_copy(told, told, meta_send_sem).wait()
+    for i in range((n - 1) * groups - ahead, (n - 1) * groups):
+        data_copy(*turn_of(i), me).wait_send()
+    for o in range(1, n):
+        for copy in meta_copies(o, me):
+            copy.wait_send()
 
 
 def shards(object_field, probe_field, intensity, positions, owner_tile):
@@ -276,52 +341,49 @@
     count, extent = intensity.shape[0], probe_field.shape[1]
     tile = object_field.shape[1]
     cap = min(count, 2 * count // n)
-    batch = min(cap, 4)
+    batch = min(cap, 2)
     members = n * stripes * subs
     rows = max(8, 2 * extent // members)
     owners = 2 * extent // rows
 
-    owner = owner_tile[:, 0]
-    places = jnp.arange(count, dtype=jnp.int32)
-    rank = jnp.sum((owner[:, None] == owner[None, :]) & (places[None, :] < places[:, None]), axis=1, dtype=jnp.int32)
-    named = jnp.arange(n, dtype=jnp.int32)[:, None, None, None] == owner
-    ranked = jnp.arange(cap, dtype=jnp.int32)[:, None] == rank
-    facts = jnp.stack([places, positions[:, 0], positions[:, 1], jnp.ones_like(places)])[:, None, :]
-    table = jnp.sum(jnp.where(named & ranked, facts, 0), axis=3, dtype=jnp.int32).reshape(n, 1, 4 * cap)
-    table = jnp.pad(table, ((0, 0), (0, 0), (0, 128 - 4 * cap)))
-
-    offsets = sorted(range(n), key=lambda o: (o != 0, o))
+    hbm = pl.BlockSpec(memory_space=pltpu.HBM)
     vmem = pl.BlockSpec(memory_space=pltpu.VMEM)
     dma = pltpu.SemaphoreType.DMA
     f32 = jnp.float32
     grad, probe_grad = pl.pallas_call(
-        functools.partial(kernel, (n, stripes, subs, cap, batch, tuple(offsets))),
+        functools.partial(kernel, (n, stripes, subs, cap, batch)),
         out_shape=(
             jax.ShapeDtypeStruct((2, tile, tile), f32),
             jax.ShapeDtypeStruct((2 * extent, extent), f32),
         ),
-        in_specs=[pl.BlockSpec(memory_space=pltpu.SMEM)] + [vmem] * 5,
+        in_specs=[hbm] * 6,
         out_specs=(vmem, vmem),
         scratch_shapes=[
+            pltpu.VMEM(intensity.shape, f32),
+            pltpu.VMEM(probe_field.shape, f32),
+            pltpu.VMEM((2, extent, extent), f32),
+            pltpu.VMEM((4, 2 * extent, 2 * extent), jnp.bfloat16),
             pltpu.VMEM((n, cap, extent, extent), f32),
             pltpu.VMEM((n, cap, extent, extent), f32),
-            pltpu.VMEM((n, 1, 128), jnp.int32),
-            pltpu.SMEM((n, 1, 128), jnp.int32),
+            pltpu.VMEM((n, 2, count), jnp.int32),
+            pltpu.VMEM((n, 1, count), jnp.int32),
+            pltpu.SMEM((n, 2, count), jnp.int32),
+            pltpu.SMEM((n, 1, count), jnp.int32),
             pltpu.VMEM((2, tile // extent, tile, extent), f32),
             pltpu.VMEM((batch, 2, tile // extent, 2 * tile - extent, extent), f32),
             pltpu.VMEM((2 * extent, extent), f32),
             pltpu.VMEM((rows, extent), f32),
             pltpu.VMEM((owners, rows, extent), f32),
             pltpu.VMEM((members - 1, rows, extent), f32),
-            dma, dma((n, cap // batch)), dma, dma((n,)), dma, dma, dma, dma, dma,
+            dma((3 + tile // extent,)), dma((n, cap // batch)), dma((n, cap // batch)), dma((2, n)), dma((2, n)), dma((2,)), dma, dma, dma, dma,
         ],
         compiler_params=pltpu.CompilerParams(
-            collective_id=0, has_side_effects=True, vmem_limit_bytes=40 * 1024 * 1024
+            collective_id=0, has_side_effects=True, vmem_limit_bytes=64 * 1024 * 1024
         ),
         cost_estimate=pl.CostEstimate(
             flops=3 * 4 * 2 * 256 * 256 * 128 * n * cap, bytes_accessed=8 * 1024 * 1024, transcendentals=0
         ),
-    )(table, table, intensity, object_field, probe_field, jnp.asarray(tables(extent)))
+    )(positions.T, owner_tile.T, intensity, object_field, probe_field, jnp.asarray(tables(extent)))
     return grad, probe_grad.reshape(2, extent, extent)
 
 

time: 79.1 us -> 70.4 us (0.89)
  local copies, waits for them, and re-layouts: 7.16 us -> 2.56 us
  Pallas kernels: 70.3 us -> 67 us
    unnamed x14 -> x4, local copies, waits for them, and re-layouts: 6.99 us -> 2.56 us
    pallas_call x1, Pallas kernels: 70.3 us -> 67 us  [shards(): pl.pallas_call(functools.partial(kernel, (n, stripes, subs, cap, batch)),...]
where the time goes in v2:
time: 70.4 us; the launch traced here: 70.3 us
  Pallas kernels  67 us (95%)
  local copies, waits for them, and re-layouts  2.56 us (4%)
    pallas_call x1, Pallas kernels, shards(): pl.pallas_call(functools.partial(kernel, (n, stripes, subs, cap, batch)),...  67 us
    unnamed x4, local copies, waits for them, and re-layouts  2.56 us

profile of v2, /device:TPU:0, one launch (start us, length us, event | category | flops | bytes accessed | tf_op | source)
XLA Modules:
  0.0 70.3 jit_solution(4422691812117945657)
XLA Ops:
  0.6 67.0 %shard_map.77 = (f32[2,256,256]{2,1,0:T(8,128)}, f32[256,128]{1,0:T(8,128)}) custom-call(s32[2,16]{1,0:T(2,128)} %bitcast.4, s32[1,16]{1,0:T(1,128)} %bitcast.5, f32[16,128,128]{2,1,0:T(8,128)} %inten_hbm.1, f32[2,256,256]{2,1,0:T(8,128)} %obj.1, f32[2,128,128]{2,1,0:T(8,128)} %probe_hbm.1, f32[2,128,128]{2,1,0:T(8,128)} %constant.2.clone.waves_hbm), custom_call_target="tpu_custom_call" | custom-call | flops 6442450944 | bytes 8388608 | tf_op jit(solution)/shard_map/pallas_call | solution.py:353
  67.7 0.0 copy-start
  67.7 1.9 %copy.10 = f32[2,256,256]{2,1,0:T(8,128)} copy(f32[2,256,256]{2,1,0:T(8,128)} %get-tuple-element.8) | data formatting | bytes 1048576
  69.6 0.0 copy-done
  69.6 0.7 copy.11
Async XLA Ops:
  67.7 1.9 %copy-start = (f32[256,128]{1,0:T(8,128)S(1)}, f32[256,128]{1,0:T(8,128)}, u32[]{:S(2)}) copy-start(f32[256,128]{1,0:T(8,128)} %get-tuple-element.5) | copy-start | bytes 393220

commit v3 on v2

--- a/solution.py
+++ b/solution.py
@@ -10,7 +10,7 @@
 from jax.sharding import PartitionSpec as P
 
 MESH = pl.DeviceIdType.MESH
-AHEAD = 4
+AHEAD = 3
 
 
 def tables(extent):
@@ -49,8 +49,8 @@
 
 
 def kernel(
-    sizes, places_hbm, owner_hbm, inten_hbm, obj, probe_hbm, waves_hbm, grad, probe_out,
-    inten, probe, waves, dft, send, recv, places_in, owner_in, places, owner, field, pad, total, reduced, gathered, arrived,
+    sizes, places_hbm, owner_hbm, inten_hbm, obj, probe_hbm, waves_hbm, grad_hbm, probe_out,
+    grad, inten, probe, waves, dft, send, recv, places_in, owner_in, places, owner, field, pad, total, reduced, gathered, arrived,
     in_sem, send_sem, recv_sem, meta_send_sem, meta_recv_sem, local_sem,
     rs_send, rs_recv, ag_send, ag_recv,
 ):
@@ -133,25 +133,30 @@
         ]
 
     targets = [other_place(me, o, n) for o in range(n)]
-    ahead = min(AHEAD, (n - 1) * groups)
-
-    def turn_of(i):
-        return 1 + (i + 1) % (n - 1), i // (n - 1)
+    total_steps = n // 2 * groups
+
+    def pair_of(i):
+        return [(i // groups * 2 + side, i % groups) for side in range(2)]
 
     for copy in own:
         copy.wait()
     fetch.wait()
-    pack(*turn_of(0), targets[turn_of(0)[0]], send)
+    early = [(1, g) for g in range(groups)]
+    queue = [turn for i in range(groups, total_steps) for turn in pair_of(i)]
+    early = [turn for turns in zip(queue, early) for turn in turns]
+    first = early + [turn for turn in queue[:2 * AHEAD] if turn not in early]
+    late = [turn for turn in queue if turn not in first]
+    pack(*first[0][:2], targets[first[0][0]], send)
     pl.semaphore_wait(barrier, members - 1)
     for o in range(1, n):
         for copy in meta_copies(o, targets[o]):
             copy.start()
-    for i in range((n - 1) * groups):
-        o, g = turn_of(i)
-        if i:
+    for o, g in first:
+        if (o, g) != first[0]:
             pack(o, g, targets[o], send)
-        if i < ahead:
-            data_copy(o, g, targets[o]).start()
+        data_copy(o, g, targets[o]).start()
+    for o, g in late:
+        pack(o, g, targets[o], send)
     for g in range(groups):
         pack(0, g, me, recv)
     for copy in later:
@@ -167,38 +172,39 @@
     pad[...] = jnp.zeros_like(pad)
 
     def step_of(j, carry):
-        i = j - groups
-        o = jnp.where(i < 0, 0, 1 + (i + 1) % (n - 1))
-        g = jnp.where(i < 0, j, i // (n - 1))
-
-        @pl.when((i >= 0) & (i + ahead < (n - 1) * groups))
+        pair = j // groups
+        g = j % groups
+
+        @pl.when((j >= groups) & (j + AHEAD < total_steps))
         def _():
-            data_copy(o, g, me).wait_send()
-            next_o, next_g = turn_of(i + ahead)
-            to = other_place(me, next_o, n)
-            data_copy(next_o, next_g, to).start()
-
-        @pl.when((o > 0) & (g == 0))
-        def _():
-            for copy in meta_copies(o, me):
-                copy.wait_recv()
-            down = [
-                pltpu.make_async_copy(places_in.at[o], places.at[o], local_sem.at[0]),
-                pltpu.make_async_copy(owner_in.at[o], owner.at[o], local_sem.at[1]),
-            ]
-            for copy in down:
-                copy.start()
-            for copy in down:
-                copy.wait()
-
-        @pl.when(o > 0)
-        def _():
+            for turn in pair_of(j):
+                data_copy(*turn, me).wait_send()
+            for o, later_g in pair_of(j + AHEAD):
+                data_copy(o, later_g, other_place(me, o, n)).start()
+
+        def settle(o):
+            @pl.when(g == 0)
+            def _():
+                for copy in meta_copies(o, me):
+                    copy.wait_recv()
+                down = [
+                    pltpu.make_async_copy(places_in.at[o], places.at[o], local_sem.at[0]),
+                    pltpu.make_async_copy(owner_in.at[o], owner.at[o], local_sem.at[1]),
+                ]
+                for copy in down:
+                    copy.start()
+                for copy in down:
+                    copy.wait()
+
             data_copy(o, g, me).wait_recv()
+
+        pl.when(pair > 0)(lambda: settle(pair * 2))
+        settle(pair * 2 + 1)
 
         corners, crops, exits = [], [], []
         pr, pi = probe[0], probe[1]
-        for b in range(batch):
-            slot = g * batch + b
+        turns = [(pair * 2 + b % 2, g * batch + b // 2) for b in range(2 * batch)]
+        for o, slot in turns:
             index, is_there = find(o, me, slot)
             row, col = places[o, 0, index], places[o, 1, index]
             weight = jnp.where(is_there, 1.0, 0.0).astype(jnp.float32)
@@ -218,7 +224,7 @@
             return jnp.concatenate(
                 [
                     jnp.concatenate(
-                        [x[b * extent:(b + 1) * extent, c * extent:(c + 1) * extent] for b in range(batch)], axis=1
+                        [x[b * extent:(b + 1) * extent, c * extent:(c + 1) * extent] for b in range(2 * batch)], axis=1
                     )
                     for c in range(2)
                 ],
@@ -227,7 +233,7 @@
 
         z = dot_left(dft[2], dft[3], turn(y))
         re, im = z[:extent], z[extent:]
-        measured = jnp.concatenate([recv[o, g * batch + b] for b in range(batch)], axis=1)
+        measured = jnp.concatenate([recv[o, slot] for o, slot in turns], axis=1)
         misfit = re * re + im * im - measured
         v = dot_left(dft[0], dft[1], jnp.concatenate([misfit * re, misfit * im], axis=0))
         turned = jnp.concatenate(
@@ -235,14 +241,14 @@
                 jnp.concatenate(
                     [v[c * extent:(c + 1) * extent, b * extent:(b + 1) * extent] for c in range(2)], axis=1
                 )
-                for b in range(batch)
+                for b in range(2 * batch)
             ],
             axis=0,
         )
         back = dot_right(turned, dft[2], dft[3])
         sum_re, sum_im = total[:extent], total[extent:]
         nothing = jnp.zeros((extent, tile - extent), jnp.float32)
-        for b in range(batch):
+        for b in range(2 * batch):
             row, col, weight = corners[b]
             cr, ci = crops[b]
             br = back[b * extent:(b + 1) * extent, :extent] * weight
@@ -259,12 +265,14 @@
             for start in range(0, tile, 64):
                 for h in range(halves):
                     held = grad[c, start:start + 64, h * extent:(h + 1) * extent]
-                    for b in range(batch):
+                    for b in range(2 * batch):
                         held += pad[b, c, h, pl.ds(tile - extent - corners[b][0] + start, 64), :]
                     grad[c, start:start + 64, h * extent:(h + 1) * extent] = held
         return carry
 
-    lax.fori_loop(0, n * groups, step_of, 0)
+    lax.fori_loop(0, total_steps, step_of, 0)
+    grad_copy = pltpu.make_async_copy(grad, grad_hbm, local_sem.at[0])
+    grad_copy.start()
 
     def when(condition, body):
         if owners == members:
@@ -329,8 +337,12 @@
 
     for place in range(owners):
         probe_out[place * rows:(place + 1) * rows] = gathered[place]
-    for i in range((n - 1) * groups - ahead, (n - 1) * groups):
-        data_copy(*turn_of(i), me).wait_send()
+    waited = [turn for i in range(groups, total_steps - AHEAD) for turn in pair_of(i)]
+    for o in range(1, n):
+        for g in range(groups):
+            if (o, g) not in waited:
+                data_copy(o, g, me).wait_send()
+    grad_copy.wait()
     for o in range(1, n):
         for copy in meta_copies(o, me):
             copy.wait_send()
@@ -357,8 +369,9 @@
             jax.ShapeDtypeStruct((2 * extent, extent), f32),
         ),
         in_specs=[hbm] * 6,
-        out_specs=(vmem, vmem),
+        out_specs=(hbm, vmem),
         scratch_shapes=[
+            pltpu.VMEM((2, tile, tile), f32),
             pltpu.VMEM(intensity.shape, f32),
             pltpu.VMEM(probe_field.shape, f32),
             pltpu.VMEM((2, extent, extent), f32),
@@ -370,7 +383,7 @@
             pltpu.SMEM((n, 2, count), jnp.int32),
             pltpu.SMEM((n, 1, count), jnp.int32),
             pltpu.VMEM((2, tile // extent, tile, extent), f32),
-            pltpu.VMEM((batch, 2, tile // extent, 2 * tile - extent, extent), f32),
+            pltpu.VMEM((2 * batch, 2, tile // extent, 2 * tile - extent, extent), f32),
             pltpu.VMEM((2 * extent, extent), f32),
             pltpu.VMEM((rows, extent), f32),
             pltpu.VMEM((owners, rows, extent), f32),

time: 70.4 us -> 67.9 us (0.964)
  Pallas kernels: 67 us -> 64.5 us
    pallas_call x1, Pallas kernels: 67 us -> 64.5 us  [shards(): pl.pallas_call(functools.partial(kernel, (n, stripes, subs, cap, batch)),...]
where the time goes in v3:
time: 67.9 us; the launch traced here: 67.7 us
  Pallas kernels  64.5 us (95%)
  local copies, waits for them, and re-layouts  2.56 us (4%)
    pallas_call x1, Pallas kernels, shards(): pl.pallas_call(functools.partial(kernel, (n, stripes, subs, cap, batch)),...  64.5 us
    unnamed x4, local copies, waits for them, and re-layouts  2.56 us

profile of v3, /device:TPU:0, one launch (start us, length us, event | category | flops | bytes accessed | tf_op | source)
XLA Modules:
  0.0 67.7 jit_solution(9280295485329002695)
XLA Ops:
  0.6 64.5 %shard_map.77 = (f32[2,256,256]{2,1,0:T(8,128)}, f32[256,128]{1,0:T(8,128)}) custom-call(s32[2,16]{1,0:T(2,128)} %bitcast.4, s32[1,16]{1,0:T(1,128)} %bitcast.5, f32[16,128,128]{2,1,0:T(8,128)} %inten_hbm.1, f32[2,256,256]{2,1,0:T(8,128)} %obj.1, f32[2,128,128]{2,1,0:T(8,128)} %probe_hbm.1, f32[2,128,128]{2,1,0:T(8,128)} %constant.2.clone.waves_hbm), custom_call_target="tpu_custom_call" | custom-call | flops 6442450944 | bytes 8388608 | tf_op jit(solution)/shard_map/pallas_call | solution.py:365
  65.2 0.0 copy-start
  65.2 1.9 %copy.10 = f32[2,256,256]{2,1,0:T(8,128)} copy(f32[2,256,256]{2,1,0:T(8,128)} %get-tuple-element.8) | data formatting | bytes 1048576
  67.1 0.0 copy-done
  67.1 0.7 copy.11
Async XLA Ops:
  65.2 1.9 %copy-start = (f32[256,128]{1,0:T(8,128)S(1)}, f32[256,128]{1,0:T(8,128)}, u32[]{:S(2)}) copy-start(f32[256,128]{1,0:T(8,128)} %get-tuple-element.5) | copy-start | bytes 393220
